TPU v7x, 32 devices: a whole 2x2x4 slice. The times are simulated.
32 devices in a mesh: groups: 2 (over y), coord: 4 (over z), ex: 4 (over x, core).
Axes of the slice: x: 2, y: 2, z: 4, core: 2. Of those that a mesh axis runs over, the one named last changes fastest.
Arguments:
- gradients: bfloat16 [768, 8192], P(('groups', 'ex'), 'coord'), parts along dimension 0, may hold values from -6 to 6
- hash_salt: int32 [2], P('groups'), parts along dimension 0, may hold values from 1 to 1073741823
- slab_offset: int32 [2], P('groups'), parts along dimension 0, may hold values from 0 to 16777215
Outputs:
- features: bfloat16 [8192, 768], P('coord', ('groups', 'ex')), parts along dimension 1
- kernel: float32 [768, 384], P(('groups', 'coord'), 'ex'), parts along dimension 0
There are 2 independent parts, one for each index of `groups`. A program takes and returns all parts, laid end to end along the dimension named above; each array names one. Nothing has to cross between parts.
All inputs are finite; a program needn't handle non-finite values.
Results may differ from a plain program's by a relative error of at most 0.0085.
Values may be sent and summed in bfloat16 or wider, within the bound.
A program may use at most 64 MiB of HBM per device.

v0:
```python
import math

import jax
import jax.numpy as jnp
from jax import lax
from jax.sharding import PartitionSpec as P

FEATS = 8192


def sign_block(coord_ids, first_col, block_width, salt_value):
    feature_ids = first_col + jnp.arange(block_width, dtype=jnp.int32)[:, None]
    mixed = coord_ids[None, :] * 2654435 ^ feature_ids * 97001 ^ salt_value
    mixed = mixed ^ lax.shift_right_logical(mixed, jnp.int32(15))
    mixed = mixed * 73244475
    mixed = mixed ^ lax.shift_right_logical(mixed, jnp.int32(13))
    mixed = mixed * 1274126177
    mixed = mixed ^ lax.shift_right_logical(mixed, jnp.int32(16))
    return 1 - 2 * (lax.shift_right_logical(mixed, jnp.int32(9)) & 1)


def shards(gradients, hash_salt, slab_offset):
    ex_local = gradients.shape[0]
    coord_local = gradients.shape[1]
    coord_parts = lax.axis_size("coord")
    coord_place = lax.axis_index("coord")
    coord_ids = (
        slab_offset[0] + coord_place * coord_local + jnp.arange(coord_local, dtype=jnp.int32)
    )
    feat_rows = FEATS // coord_parts
    block_width = math.gcd(FEATS, 512)
    starts = 0 + jnp.arange(FEATS // block_width, dtype=jnp.int32) * block_width

    def one_block(first_col):
        signs = sign_block(coord_ids, first_col, block_width, hash_salt[0]).astype(jnp.bfloat16)
        return lax.dot_general(
            signs, gradients, (((1,), (1,)), ((), ())), preferred_element_type=jnp.float32
        )

    totals = lax.psum(lax.map(one_block, starts).reshape(FEATS, ex_local), "coord")
    own_sums = lax.dynamic_slice_in_dim(totals, coord_place * feat_rows, feat_rows, 0)
    features = (own_sums / math.sqrt(coord_local * coord_parts)).astype(jnp.bfloat16)
    gathered = lax.all_gather(features, "ex", axis=1, tiled=True)
    kernel = lax.psum_scatter(
        (
            lax.dot_general(
                gathered, features, (((0,), (0,)), ((), ())), preferred_element_type=jnp.float32
            )
            / FEATS
        ).astype(jnp.bfloat16),
        "coord",
        scatter_dimension=0,
        tiled=True,
    ).astype(jnp.float32)
    return (features, kernel)


def solution(mesh):
    return jax.shard_map(
        shards,
        mesh=mesh,
        in_specs=(P(("groups", "ex"), "coord"), P("groups"), P("groups")),
        out_specs=(P("coord", ("groups", "ex")), P(("groups", "coord"), "ex")),
        check_vma=False,
    )
```

profile of v0, /device:TPU:0, one launch (start us, length us, event | category | flops | bytes accessed | tf_op | source)
XLA Modules:
  0.0 300.6 jit_solution(2803641542246928210)
XLA Ops:
  7.9 114.1 %while.11 = (s32[]{:T(128)}, f32[16,512,96]{1,0,2:T(8,128)S(1)}, s32[16]{0:T(128)S(1)}, s32[1]{0:T(128)}, bf16[96,2048]{1,0:T(8,128)(2,1)}, /*index=5*/s32[]{:T(128)}, s32[]{:T(128)}, s32[]{:T(128)}) while((s32[]{:T(128)}, f32[16,512,96]{1,0,2:T(8,128)S(1)}, s32[16]{0:T(128)S(1)}, s32[1]{0:T(128)}, bf16[96,2048]{1,0:T(8,128)(2,1)}, ...), condition=%wide.region_1.2_spmd.clone, body=%wide.region_0.1_spmd.clone.sunk | while | flops 217060352 | bytes 1396849 | solution.py:40
  7.9 0.6 dynamic_slice.11
  8.5 0.6 add_multiply_fusion.4
  9.1 4.0 %fusion.31 = f32[1,512,96]{1,2,0:T(8,128)S(1)} fusion(bf16[96,2048]{1,0:T(8,128)(2,1)} %get-tuple-element.119, s32[]{:T(128)} %bitcast.18, s32[512]{0:T(512)S(1)} %add_multiply_fusion.4, s32[2048]{0:T(1024)S(1)} %add_multiply_fusion.5), kind=kOutput, calls=%fused_computation.12.clone.1 | convolution fusion | flops 217055232 | bytes 600068 | tf_op jit(solution)/shard_map/while/body/eval_jaxpr/dot_general | solution.py:36
  13.3 1.7 dynamic_update_slice.6
  15.0 0.6 dynamic_slice.11
  15.6 0.6 add_multiply_fusion.4
  16.3 4.0 %fusion.31 = f32[1,512,96]{1,2,0:T(8,128)S(1)} fusion(bf16[96,2048]{1,0:T(8,128)(2,1)} %get-tuple-element.119, s32[]{:T(128)} %bitcast.18, s32[512]{0:T(512)S(1)} %add_multiply_fusion.4, s32[2048]{0:T(1024)S(1)} %add_multiply_fusion.5), kind=kOutput, calls=%fused_computation.12.clone.1 | convolution fusion | flops 217055232 | bytes 600068 | tf_op jit(solution)/shard_map/while/body/eval_jaxpr/dot_general | solution.py:36
  20.4 1.7 dynamic_update_slice.6
  22.2 0.6 dynamic_slice.11
  22.8 0.6 add_multiply_fusion.4
  23.4 4.0 %fusion.31 = f32[1,512,96]{1,2,0:T(8,128)S(1)} fusion(bf16[96,2048]{1,0:T(8,128)(2,1)} %get-tuple-element.119, s32[]{:T(128)} %bitcast.18, s32[512]{0:T(512)S(1)} %add_multiply_fusion.4, s32[2048]{0:T(1024)S(1)} %add_multiply_fusion.5), kind=kOutput, calls=%fused_computation.12.clone.1 | convolution fusion | flops 217055232 | bytes 600068 | tf_op jit(solution)/shard_map/while/body/eval_jaxpr/dot_general | solution.py:36
  27.6 1.7 dynamic_update_slice.6
  29.3 0.6 dynamic_slice.11
  29.9 0.6 add_multiply_fusion.4
  30.5 4.0 %fusion.31 = f32[1,512,96]{1,2,0:T(8,128)S(1)} fusion(bf16[96,2048]{1,0:T(8,128)(2,1)} %get-tuple-element.119, s32[]{:T(128)} %bitcast.18, s32[512]{0:T(512)S(1)} %add_multiply_fusion.4, s32[2048]{0:T(1024)S(1)} %add_multiply_fusion.5), kind=kOutput, calls=%fused_computation.12.clone.1 | convolution fusion | flops 217055232 | bytes 600068 | tf_op jit(solution)/shard_map/while/body/eval_jaxpr/dot_general | solution.py:36
  34.7 1.7 dynamic_update_slice.6
  36.4 0.6 dynamic_slice.11
  37.0 0.6 add_multiply_fusion.4
  37.7 4.0 %fusion.31 = f32[1,512,96]{1,2,0:T(8,128)S(1)} fusion(bf16[96,2048]{1,0:T(8,128)(2,1)} %get-tuple-element.119, s32[]{:T(128)} %bitcast.18, s32[512]{0:T(512)S(1)} %add_multiply_fusion.4, s32[2048]{0:T(1024)S(1)} %add_multiply_fusion.5), kind=kOutput, calls=%fused_computation.12.clone.1 | convolution fusion | flops 217055232 | bytes 600068 | tf_op jit(solution)/shard_map/while/body/eval_jaxpr/dot_general | solution.py:36
  41.8 1.7 dynamic_update_slice.6
  43.6 0.6 dynamic_slice.11
  44.2 0.6 add_multiply_fusion.4
  44.8 4.0 %fusion.31 = f32[1,512,96]{1,2,0:T(8,128)S(1)} fusion(bf16[96,2048]{1,0:T(8,128)(2,1)} %get-tuple-element.119, s32[]{:T(128)} %bitcast.18, s32[512]{0:T(512)S(1)} %add_multiply_fusion.4, s32[2048]{0:T(1024)S(1)} %add_multiply_fusion.5), kind=kOutput, calls=%fused_computation.12.clone.1 | convolution fusion | flops 217055232 | bytes 600068 | tf_op jit(solution)/shard_map/while/body/eval_jaxpr/dot_general | solution.py:36
  49.0 1.7 dynamic_update_slice.6
  50.7 0.6 dynamic_slice.11
  51.3 0.6 add_multiply_fusion.4
  51.9 4.0 %fusion.31 = f32[1,512,96]{1,2,0:T(8,128)S(1)} fusion(bf16[96,2048]{1,0:T(8,128)(2,1)} %get-tuple-element.119, s32[]{:T(128)} %bitcast.18, s32[512]{0:T(512)S(1)} %add_multiply_fusion.4, s32[2048]{0:T(1024)S(1)} %add_multiply_fusion.5), kind=kOutput, calls=%fused_computation.12.clone.1 | convolution fusion | flops 217055232 | bytes 600068 | tf_op jit(solution)/shard_map/while/body/eval_jaxpr/dot_general | solution.py:36
  56.1 1.7 dynamic_update_slice.6
  58.4 0.6 add_multiply_fusion.4
  59.1 4.0 %fusion.31 = f32[1,512,96]{1,2,0:T(8,128)S(1)} fusion(bf16[96,2048]{1,0:T(8,128)(2,1)} %get-tuple-element.119, s32[]{:T(128)} %bitcast.18, s32[512]{0:T(512)S(1)} %add_multiply_fusion.4, s32[2048]{0:T(1024)S(1)} %add_multiply_fusion.5), kind=kOutput, calls=%fused_computation.12.clone.1 | convolution fusion | flops 217055232 | bytes 600068 | tf_op jit(solution)/shard_map/while/body/eval_jaxpr/dot_general | solution.py:36
  63.2 1.7 dynamic_update_slice.6
  65.6 0.6 add_multiply_fusion.4
  66.2 4.0 %fusion.31 = f32[1,512,96]{1,2,0:T(8,128)S(1)} fusion(bf16[96,2048]{1,0:T(8,128)(2,1)} %get-tuple-element.119, s32[]{:T(128)} %bitcast.18, s32[512]{0:T(512)S(1)} %add_multiply_fusion.4, s32[2048]{0:T(1024)S(1)} %add_multiply_fusion.5), kind=kOutput, calls=%fused_computation.12.clone.1 | convolution fusion | flops 217055232 | bytes 600068 | tf_op jit(solution)/shard_map/while/body/eval_jaxpr/dot_general | solution.py:36
  70.4 1.7 dynamic_update_slice.6
  72.7 0.6 add_multiply_fusion.4
  73.3 4.0 %fusion.31 = f32[1,512,96]{1,2,0:T(8,128)S(1)} fusion(bf16[96,2048]{1,0:T(8,128)(2,1)} %get-tuple-element.119, s32[]{:T(128)} %bitcast.18, s32[512]{0:T(512)S(1)} %add_multiply_fusion.4, s32[2048]{0:T(1024)S(1)} %add_multiply_fusion.5), kind=kOutput, calls=%fused_computation.12.clone.1 | convolution fusion | flops 217055232 | bytes 600068 | tf_op jit(solution)/shard_map/while/body/eval_jaxpr/dot_general | solution.py:36
  77.5 1.7 dynamic_update_slice.6
  79.8 0.6 add_multiply_fusion.4
  80.5 4.0 %fusion.31 = f32[1,512,96]{1,2,0:T(8,128)S(1)} fusion(bf16[96,2048]{1,0:T(8,128)(2,1)} %get-tuple-element.119, s32[]{:T(128)} %bitcast.18, s32[512]{0:T(512)S(1)} %add_multiply_fusion.4, s32[2048]{0:T(1024)S(1)} %add_multiply_fusion.5), kind=kOutput, calls=%fused_computation.12.clone.1 | convolution fusion | flops 217055232 | bytes 600068 | tf_op jit(solution)/shard_map/while/body/eval_jaxpr/dot_general | solution.py:36
  84.6 1.7 dynamic_update_slice.6
  87.0 0.6 add_multiply_fusion.4
  87.6 4.0 %fusion.31 = f32[1,512,96]{1,2,0:T(8,128)S(1)} fusion(bf16[96,2048]{1,0:T(8,128)(2,1)} %get-tuple-element.119, s32[]{:T(128)} %bitcast.18, s32[512]{0:T(512)S(1)} %add_multiply_fusion.4, s32[2048]{0:T(1024)S(1)} %add_multiply_fusion.5), kind=kOutput, calls=%fused_computation.12.clone.1 | convolution fusion | flops 217055232 | bytes 600068 | tf_op jit(solution)/shard_map/while/body/eval_jaxpr/dot_general | solution.py:36
  91.8 1.7 dynamic_update_slice.6
  94.1 0.6 add_multiply_fusion.4
  94.7 4.0 %fusion.31 = f32[1,512,96]{1,2,0:T(8,128)S(1)} fusion(bf16[96,2048]{1,0:T(8,128)(2,1)} %get-tuple-element.119, s32[]{:T(128)} %bitcast.18, s32[512]{0:T(512)S(1)} %add_multiply_fusion.4, s32[2048]{0:T(1024)S(1)} %add_multiply_fusion.5), kind=kOutput, calls=%fused_computation.12.clone.1 | convolution fusion | flops 217055232 | bytes 600068 | tf_op jit(solution)/shard_map/while/body/eval_jaxpr/dot_general | solution.py:36
  98.9 1.7 dynamic_update_slice.6
  100.6 0.6 dynamic_slice.11
  101.2 0.6 add_multiply_fusion.4
  101.9 4.0 %fusion.31 = f32[1,512,96]{1,2,0:T(8,128)S(1)} fusion(bf16[96,2048]{1,0:T(8,128)(2,1)} %get-tuple-element.119, s32[]{:T(128)} %bitcast.18, s32[512]{0:T(512)S(1)} %add_multiply_fusion.4, s32[2048]{0:T(1024)S(1)} %add_multiply_fusion.5), kind=kOutput, calls=%fused_computation.12.clone.1 | convolution fusion | flops 217055232 | bytes 600068 | tf_op jit(solution)/shard_map/while/body/eval_jaxpr/dot_general | solution.py:36
  106.0 1.7 dynamic_update_slice.6
  108.4 0.6 add_multiply_fusion.4
  109.0 4.0 %fusion.31 = f32[1,512,96]{1,2,0:T(8,128)S(1)} fusion(bf16[96,2048]{1,0:T(8,128)(2,1)} %get-tuple-element.119, s32[]{:T(128)} %bitcast.18, s32[512]{0:T(512)S(1)} %add_multiply_fusion.4, s32[2048]{0:T(1024)S(1)} %add_multiply_fusion.5), kind=kOutput, calls=%fused_computation.12.clone.1 | convolution fusion | flops 217055232 | bytes 600068 | tf_op jit(solution)/shard_map/while/body/eval_jaxpr/dot_general | solution.py:36
  113.2 1.7 dynamic_update_slice.6
  115.5 0.6 add_multiply_fusion.4
  116.1 4.0 %fusion.31 = f32[1,512,96]{1,2,0:T(8,128)S(1)} fusion(bf16[96,2048]{1,0:T(8,128)(2,1)} %get-tuple-element.119, s32[]{:T(128)} %bitcast.18, s32[512]{0:T(512)S(1)} %add_multiply_fusion.4, s32[2048]{0:T(1024)S(1)} %add_multiply_fusion.5), kind=kOutput, calls=%fused_computation.12.clone.1 | convolution fusion | flops 217055232 | bytes 600068 | tf_op jit(solution)/shard_map/while/body/eval_jaxpr/dot_general | solution.py:36
  120.3 1.7 dynamic_update_slice.6
  122.0 4.0 %copy.8 = f32[12,8,16,512]{3,1,2,0:T(8,128)} copy(f32[12,8,16,512]{3,2,1,0:T(8,128)S(1)} %bitcast.22) | data formatting | bytes 6291456
  126.0 123.9 %all-reduce.2.cloned.1.call-done = f32[8192,96]{0,1:T(8,128)} async-done(((f32[8192,96]{0,1:T(8,128)}), f32[8192,96]{0,1:T(8,128)}) %all-reduce.2.cloned.1.call-update) | async-done | bytes 3145744 | tf_op jit(solution)/shard_map/psum | solution.py:40
  249.9 1.9 multiply_convert_fusion
  251.9 18.8 %all-gather.2.cloned.1.call-done = bf16[2048,384]{0,1:T(8,128)(2,1)} async-done(((bf16[2048,96]{0,1:T(8,128)(2,1)}), bf16[2048,384]{0,1:T(8,128)(2,1)}) %all-gather.2.cloned.1.call-update) | async-done | bytes 1572880 | tf_op jit(solution)/shard_map/all_gather | solution.py:43
  270.8 2.7 fusion.22
  273.5 19.2 %reduce-scatter.2.cloned.1.call-done = bf16[96,96]{1,0:T(8,128)(2,1)} async-done(((bf16[384,96]{1,0:T(8,128)(2,1)}), bf16[96,96]{1,0:T(8,128)(2,1)}) %reduce-scatter.2.cloned.1.call-update) | async-done | bytes 18448 | tf_op jit(solution)/shard_map/reduce_scatter | solution.py:44
  292.7 1.4 convert_element_type.14
  (48 shorter events, 8.3 us)
Async XLA Ops:
  7.2 242.8 %all-reduce.2.cloned.1.call-start = ((), (), s32[]{:S(2)}) async-start(), calls=%async_computation.1 | async-start | bytes 6291456 | tf_op jit(solution)/shard_map/psum | solution.py:40
  126.0 144.8 %all-gather.2.cloned.1.call-start = ((), (), s32[]{:S(2)}) async-start(), calls=%async_computation.2 | async-start | bytes 1966080 | tf_op jit(solution)/shard_map/all_gather | solution.py:43
  251.9 40.8 %reduce-scatter.2.cloned.1.call-start = ((), (), s32[]{:S(2)}) async-start(), calls=%async_computation.3 | async-start | bytes 122880 | tf_op jit(solution)/shard_map/reduce_scatter | solution.py:44
Sparse Core Ops, SparseCore 0:
  126.1 123.7 all-reduce.1
  252.1 18.6 all-gather.1
  273.6 19.0 reduce-scatter.1
where the time goes:
time: 302 us; the launch traced here: 301 us
  waiting for transfers between devices  162 us (54%)
  matrix products  66.1 us (22%)
  local copies, waits for them, and re-layouts  43.9 us (15%)
  between operations  14.4 us (5%)
  other arithmetic  13.3 us (4%)
    psum x1, waiting for transfers between devices, shards(): lax.psum(lax.map(one_block, starts).reshape(FEATS, ex_local), 'coord')  124 us
    dot_general x16, matrix products, one_block(): lax.dot_general(signs, gradients, (((1,), (1,)), ((), ())), preferred_ele...  63.4 us
    dynamic_update_slice x32, local copies, waits for them, and re-layouts, shards(): lax.map(one_block, starts).reshape(FEATS, ex_local)  30.4 us
    reduce_scatter x1, waiting for transfers between devices, shards(): lax.psum_scatter((lax.dot_general(gathered, features, (((0,), (0,)), ((),...  19.2 us
    all_gather x1, waiting for transfers between devices, shards(): gathered = lax.all_gather(features, 'ex', axis=1, tiled=True)  18.8 us
    mul x32, other arithmetic, sign_block(): mixed = coord_ids[None, :] * 2654435 ^ feature_ids * 97001 ^ salt_value  10 us
    dynamic_slice x16, local copies, waits for them, and re-layouts, shards(): lax.map(one_block, starts).reshape(FEATS, ex_local)  9.52 us
  transfers between devices with their start and end apart: 3, of which 3 were waited for; matrix products, arithmetic and copies ran while one was open for 0% of the time, Pallas kernels for 0%

commit v1 on v0

v1 whole, which is shorter than its diff:
```python
import functools
import math

import jax
import jax.numpy as jnp
import numpy as np
from jax import lax
from jax.experimental import pallas as pl
from jax.experimental.pallas import tpu as pltpu
from jax.sharding import PartitionSpec as P

FEATS = 8192
LAST = int(np.array((1274126177 << 6) & 0xFFFFFFFF, np.uint32).astype(np.int32))


def sign_tile(coord_term, feat_term):
    m = coord_term ^ feat_term
    m = m ^ lax.shift_right_logical(m, jnp.int32(15))
    m = m * jnp.int32(73244475)
    m = m ^ lax.shift_right_logical(m, jnp.int32(13))
    p = m * jnp.int32(LAST)
    p = p ^ (p << 16)
    return jnp.where(p < 0, -1.0, 1.0).astype(jnp.bfloat16)


def project_kernel(sub, feat_rows, block, salt_ref, first_ref, place_ref, grads_ref, out_ref, signs, coord_term):
    coords = grads_ref.shape[1]
    step = pl.program_id(0)

    @pl.when(step == 0)
    def _():
        ids = first_ref[0] + lax.broadcasted_iota(jnp.int32, (16, coords), 1)
        coord_term[...] = (ids * 2654435) ^ salt_ref[0]

    @pl.loop(0, block // 16)
    def _(i):
        row = step * block + i * 16
        feat = (row // sub) * feat_rows + place_ref[0] * sub + row % sub
        feat_term = (feat + lax.broadcasted_iota(jnp.int32, (16, 128), 0)) * 97001
        for j in range(coords // 128):
            signs[pl.ds(pl.multiple_of(i * 16, 16), 16), pl.ds(j * 128, 128)] = sign_tile(
                coord_term[:, pl.ds(j * 128, 128)], feat_term
            )

    out_ref[...] = lax.dot_general(
        signs[...], grads_ref[...], (((1,), (1,)), ((), ())), preferred_element_type=jnp.float32
    ).astype(out_ref.dtype)


def project(gathered, salt, first, place, rows, sub, feat_rows):
    examples, coords = gathered.shape
    block = 512
    return pl.pallas_call(
        functools.partial(project_kernel, sub, feat_rows, block),
        grid=(rows // block,),
        out_shape=jax.ShapeDtypeStruct((rows, examples), jnp.bfloat16),
        in_specs=[pl.BlockSpec(memory_space=pltpu.SMEM)] * 3
        + [pl.BlockSpec((examples, coords), lambda i: (0, 0))],
        out_specs=pl.BlockSpec((block, examples), lambda i: (i, 0)),
        scratch_shapes=[
            pltpu.VMEM((block, coords), jnp.bfloat16),
            pltpu.VMEM((16, coords), jnp.int32),
        ],
        compiler_params=pltpu.CompilerParams(vmem_limit_bytes=40 * 2**20),
    )(salt, first, place, gathered)


def general(gradients, hash_salt, slab_offset):
    coord_local = gradients.shape[1]
    coord_parts = lax.axis_size("coord")
    ex_parts = lax.axis_size("ex")
    examples = gradients.shape[0] * ex_parts
    ex_local = gradients.shape[0]
    feat_rows = FEATS // coord_parts
    sub = feat_rows // ex_parts
    first = slab_offset + lax.axis_index("coord") * coord_local
    place = lax.axis_index("ex").reshape(1)
    gathered = lax.all_gather(gradients, "ex", axis=0, tiled=True)
    part = project(gathered, hash_salt, first, place, FEATS // ex_parts, sub, feat_rows)
    parts = lax.all_to_all(part.reshape(coord_parts, sub, examples), "coord", 0, 0)
    sums = jnp.sum(parts.astype(jnp.float32), axis=0)
    own = (sums / math.sqrt(coord_local * coord_parts)).astype(jnp.bfloat16)
    blocks = own.reshape(sub, ex_parts, ex_local).transpose(1, 0, 2)
    features = lax.all_to_all(blocks, "ex", 0, 0).reshape(feat_rows, ex_local)
    gram = lax.dot_general(own, own, (((0,), (0,)), ((), ())), preferred_element_type=jnp.float32) / FEATS
    gram = gram.astype(jnp.bfloat16).reshape(examples, ex_parts, ex_local).transpose(1, 0, 2)
    gram = jnp.sum(lax.all_to_all(gram, "ex", 0, 0).astype(jnp.float32), axis=0)
    gram = gram.astype(jnp.bfloat16).reshape(coord_parts, examples // coord_parts, ex_local)
    kernel = jnp.sum(lax.all_to_all(gram, "coord", 0, 0).astype(jnp.float32), axis=0)
    return features, kernel


def solution(mesh):
    return jax.shard_map(
        general,
        mesh=mesh,
        in_specs=(P(("groups", "ex"), "coord"), P("groups"), P("groups")),
        out_specs=(P("coord", ("groups", "ex")), P(("groups", "coord"), "ex")),
        check_vma=False,
    )
```

time: 302 us -> 128 us (0.42)
  waiting for transfers between devices: 162 us -> 40.5 us
  matrix products: 66.1 us -> 1.12 us
  blocking collectives: 0 us -> 41.8 us
  local copies, waits for them, and re-layouts: 43.9 us -> 4.59 us
  Pallas kernels: 0 us -> 13.6 us
  other arithmetic: 13.3 us -> 0.36 us
  starting transfers between devices: 0.12 us -> 10.3 us
    psum x1 -> x0, waiting for transfers between devices: 124 us -> none  [shards(): lax.psum(lax.map(one_block, starts).reshape(FEATS, ex_local), 'coord')]
    dot_general x17 -> x1, matrix products: 66.1 us -> 1.12 us  [general(): lax.dot_general(own, own, (((0,), (0,)), ((), ())), preferred_element_typ...]
    all_to_all x0 -> x1, blocking collectives: none -> 41.8 us  [general(): lax.all_to_all(part.reshape(coord_parts, sub, examples), 'coord', 0, 0)]
    dynamic_update_slice x32 -> x0, local copies, waits for them, and re-layouts: 30.4 us -> none  [shards(): lax.map(one_block, starts).reshape(FEATS, ex_local)]
    reduce_scatter x1 -> x0, waiting for transfers between devices: 19.2 us -> none  [shards(): lax.psum_scatter((lax.dot_general(gathered, features, (((0,), (0,)), ((),...]
    all_to_all x0 -> x3, waiting for transfers between devices: none -> 17 us  [the longest x1 6.6 us: general(): features = lax.all_to_all(blocks, 'ex', 0, 0).reshape(feat_rows, ex_local)]
    pallas_call x0 -> x1, Pallas kernels: none -> 13.6 us  [project(): pl.pallas_call(functools.partial(project_kernel, sub, feat_rows, block),...]
    all_to_all x0 -> x3, starting transfers between devices: none -> 10.2 us  [the longest x1 3.46 us: general(): features = lax.all_to_all(blocks, 'ex', 0, 0).reshape(feat_rows, ex_local)]
  transfers between devices with their start and end apart: 3 -> 4, of which waited for: 3 -> 4; matrix products, arithmetic and copies ran while one was open for 0% -> 2% of each run, Pallas kernels for 0% -> 0%
where the time goes in v1:
time: 128 us
  blocking collectives  41.8 us (33%)
  waiting for transfers between devices  40.5 us (32%)
  between operations  15.4 us (12%)
  Pallas kernels  13.6 us (11%)
  starting transfers between devices  10.3 us (8%)
  local copies, waits for them, and re-layouts  4.59 us (4%)
    all_to_all x1, blocking collectives, general(): lax.all_to_all(part.reshape(coord_parts, sub, examples), 'coord', 0, 0)  41.8 us
    all_gather x1, waiting for transfers between devices, general(): gathered = lax.all_gather(gradients, 'ex', axis=0, tiled=True)  22.8 us
    pallas_call x1, Pallas kernels, project(): pl.pallas_call(functools.partial(project_kernel, sub, feat_rows, block),...  13.6 us
    all_to_all x1, waiting for transfers between devices, general(): features = lax.all_to_all(blocks, 'ex', 0, 0).reshape(feat_rows, ex_local)  6.6 us
    all_to_all x1, waiting for transfers between devices, general(): gram = jnp.sum(lax.all_to_all(gram, 'ex', 0, 0).astype(jnp.float32), axis=0)  5.41 us
    all_to_all x1, waiting for transfers between devices, general(): lax.all_to_all(gram, 'coord', 0, 0).astype(jnp.float32)  5.01 us
    all_to_all x1, starting transfers between devices, general(): features = lax.all_to_all(blocks, 'ex', 0, 0).reshape(feat_rows, ex_local)  3.46 us
    all_to_all x1, starting transfers between devices, general(): gram = jnp.sum(lax.all_to_all(gram, 'ex', 0, 0).astype(jnp.float32), axis=0)  3.45 us
  transfers between devices with their start and end apart: 4, of which 4 were waited for; matrix products, arithmetic and copies ran while one was open for 2% of the time, Pallas kernels for 0%

profile of v1, /device:TPU:0, one launch (start us, length us, event | category | flops | bytes accessed | tf_op | source)
XLA Modules:
  0.0 127.5 jit_solution(2609268541054873796)
XLA Ops:
  7.2 0.0 all-gather.2.cloned.1.call-start
  7.2 0.7 all-gather.2.cloned.1.call-update
  9.2 22.8 %all-gather.2.cloned.1.call-done.grads_ref = bf16[384,2048]{1,0:T(8,128)(2,1)} async-done(((bf16[96,2048]{1,0:T(8,128)(2,1)}), bf16[384,2048]{1,0:T(8,128)(2,1)}) %all-gather.2.cloned.1.call-update) | async-done | bytes 1572880 | tf_op jit(solution)/shard_map/all_gather | solution.py:78
  31.9 0.0 copy-start
  31.9 1.4 %copy-done = bf16[384,2048]{1,0:T(8,128)(2,1)S(1)} copy-done((bf16[384,2048]{1,0:T(8,128)(2,1)S(1)}, bf16[384,2048]{1,0:T(8,128)(2,1)}, u32[]{:S(2)}) %copy-start) | copy-done | bytes 1572888
  33.4 13.6 %shard_map.50 = bf16[2048,384]{1,0:T(8,128)(2,1)S(1)} custom-call(s32[1]{0:T(128)S(6)} %copy.15.salt_ref, s32[1]{0:T(128)S(6)} %add.7.first_ref, s32[1]{0:T(128)} %bitcast.1.place_ref, bf16[384,2048]{1,0:T(8,128)(2,1)S(1)} %copy-done), custom_call_target="tpu_custom_call" | custom-call | tf_op jit(solution)/shard_map/pallas_call | solution.py:53
  47.0 41.8 %all_to_all.20 = bf16[4,512,384]{2,1,0:T(8,128)(2,1)S(1)} all-to-all(bf16[4,512,384]{2,1,0:T(8,128)(2,1)S(1)} %bitcast.15), channel_id=1, replica_groups=mesh['groups'=2,'coord'=4,'ex'=4] {'coord'}, dimensions={0} | all-to-all | bytes 3145728 | tf_op jit(solution)/shard_map/all_to_all | solution.py:80
  88.7 0.2 convert_reduce_fusion
  88.9 0.1 multiply_convert_fusion
  89.0 1.1 fusion
  90.1 3.5 %all-to-all-start.2 = ((bf16[4,384,96]{1,2,0:T(8,128)(2,1)}), bf16[4,384,96]{1,2,0:T(8,128)(2,1)S(1)}, u32[]{:S(2)}, u32[]{:S(2)}) async-start(bf16[4,384,96]{1,2,0:T(8,128)(2,1)} %bitcast.6), calls=%async_computation.2 | async-start | bytes 589824 | tf_op jit(solution)/shard_map/all_to_all | solution.py:87
  93.6 0.9 copy.8
  94.5 5.4 %all-to-all-done.2 = bf16[4,384,96]{1,2,0:T(8,128)(2,1)S(1)} async-done(((bf16[4,384,96]{1,2,0:T(8,128)(2,1)}), bf16[4,384,96]{1,2,0:T(8,128)(2,1)S(1)}, u32[]{:S(2)}, u32[]{:S(2)}) %all-to-all-start.2) | async-done | bytes 294944 | tf_op jit(solution)/shard_map/all_to_all | solution.py:87
  100.0 3.5 %all-to-all-start.1 = ((bf16[4,512,96]{1,2,0:T(8,128)(2,1)}), bf16[4,512,96]{1,2,0:T(8,128)(2,1)S(1)}, u32[]{:S(2)}, u32[]{:S(2)}) async-start(bf16[4,512,96]{1,2,0:T(8,128)(2,1)} %bitcast.4), calls=%async_computation.1 | async-start | bytes 786432 | tf_op jit(solution)/shard_map/all_to_all | solution.py:84
  103.5 0.1 reshape.28
  103.6 0.6 copy.10
  104.2 6.6 %all-to-all-done.1 = bf16[4,512,96]{1,2,0:T(8,128)(2,1)S(1)} async-done(((bf16[4,512,96]{1,2,0:T(8,128)(2,1)}), bf16[4,512,96]{1,2,0:T(8,128)(2,1)S(1)}, u32[]{:S(2)}, u32[]{:S(2)}) %all-to-all-start.1) | async-done | bytes 393248 | tf_op jit(solution)/shard_map/all_to_all | solution.py:84
  110.8 3.3 %all-to-all-start.3 = ((bf16[4,96,96]{1,2,0:T(8,128)(2,1)}), bf16[4,96,96]{1,2,0:T(8,128)(2,1)S(1)}, u32[]{:S(2)}, u32[]{:S(2)}) async-start(bf16[4,96,96]{1,2,0:T(8,128)(2,1)} %copy.10), calls=%async_computation.3 | async-start | bytes 196608 | tf_op jit(solution)/shard_map/all_to_all | solution.py:89
  114.1 0.8 copy.14
  114.9 5.0 %all-to-all-done.3 = bf16[4,96,96]{1,2,0:T(8,128)(2,1)S(1)} async-done(((bf16[4,96,96]{1,2,0:T(8,128)(2,1)}), bf16[4,96,96]{1,2,0:T(8,128)(2,1)S(1)}, u32[]{:S(2)}, u32[]{:S(2)}) %all-to-all-start.3) | async-done | bytes 73760 | tf_op jit(solution)/shard_map/all_to_all | solution.py:89
  120.0 0.7 copy.12
  (2 shorter events, 0.1 us)
Async XLA Ops:
  7.2 24.8 %all-gather.2.cloned.1.call-start = ((), (), s32[]{:S(2)}) async-start(), calls=%async_computation.4 | async-start | bytes 1966080 | tf_op jit(solution)/shard_map/all_gather | solution.py:78
  31.9 1.4 %copy-start = (bf16[384,2048]{1,0:T(8,128)(2,1)S(1)}, bf16[384,2048]{1,0:T(8,128)(2,1)}, u32[]{:S(2)}) copy-start(bf16[384,2048]{1,0:T(8,128)(2,1)} %all-gather.2.cloned.1.call-done.grads_ref) | copy-start | bytes 4718596
  90.1 9.8 %all-to-all-start.2 = ((bf16[4,384,96]{1,2,0:T(8,128)(2,1)}), bf16[4,384,96]{1,2,0:T(8,128)(2,1)S(1)}, u32[]{:S(2)}, u32[]{:S(2)}) async-start(bf16[4,384,96]{1,2,0:T(8,128)(2,1)} %bitcast.6), calls=%async_computation.2 | async-start | bytes 589824 | tf_op jit(solution)/shard_map/all_to_all | solution.py:87
  100.0 10.9 %all-to-all-start.1 = ((bf16[4,512,96]{1,2,0:T(8,128)(2,1)}), bf16[4,512,96]{1,2,0:T(8,128)(2,1)S(1)}, u32[]{:S(2)}, u32[]{:S(2)}) async-start(bf16[4,512,96]{1,2,0:T(8,128)(2,1)} %bitcast.4), calls=%async_computation.1 | async-start | bytes 786432 | tf_op jit(solution)/shard_map/all_to_all | solution.py:84
  110.8 9.1 %all-to-all-start.3 = ((bf16[4,96,96]{1,2,0:T(8,128)(2,1)}), bf16[4,96,96]{1,2,0:T(8,128)(2,1)S(1)}, u32[]{:S(2)}, u32[]{:S(2)}) async-start(bf16[4,96,96]{1,2,0:T(8,128)(2,1)} %copy.10), calls=%async_computation.3 | async-start | bytes 196608 | tf_op jit(solution)/shard_map/all_to_all | solution.py:89
Sparse Core Ops, SparseCore 0:
  9.6 22.3 all-gather.1

commit v2 on v1

--- a/solution.py
+++ b/solution.py
@@ -90,9 +90,175 @@
     return features, kernel
 
 
+def fused_kernel(
+    salt_ref, offset_ref, grads_ref, feats_ref, kern_ref,
+    grads, signs, coord_term, part, part_in, own, feat, feat_in, gram, gram_in,
+    send_g, recv_g, send_p, recv_p, send_f, recv_f, send_k, recv_k,
+):
+    z, x = lax.axis_index("coord"), lax.axis_index("ex")
+    xc, c = x // 2, x % 2
+    zz = z % 2
+    z_pair, z_far = z + 1 - 2 * zz, (z + 2) % 4
+    oc, oz = 1 - c, 1 - zz
+    ox = 1 - xc
+    me = z * 4 + x
+    n_ex, width = grads_ref.shape
+    half = signs.shape[1]
+    feat_rows = FEATS // 4
+    sends = []
+
+    def remote(src, dst, send, recv, zt, xt):
+        return pltpu.make_async_remote_copy(
+            src_ref=src, dst_ref=dst, send_sem=send, recv_sem=recv,
+            device_id={"coord": zt, "ex": xt}, device_id_type=pl.DeviceIdType.MESH,
+        )
+
+    def start(*args):
+        copy = remote(*args)
+        copy.start()
+        sends.append(copy)
+
+    barrier = pltpu.get_barrier_semaphore()
+    for d in range(1, 16):
+        t = (me + d) % 16
+        pl.semaphore_signal(
+            barrier, inc=1, device_id={"coord": t // 4, "ex": t % 4}, device_id_type=pl.DeviceIdType.MESH
+        )
+    ids = offset_ref[0] + (z // 2) * (2 * width) + lax.broadcasted_iota(jnp.int32, (16, 2 * width), 1)
+    coord_term[...] = (ids * 2654435) ^ salt_ref[0]
+    grads[zz, xc, c] = grads_ref[...]
+    pl.semaphore_wait(barrier, 15)
+
+    mine = grads.at[zz, xc, c]
+    came = recv_g.at[zz, xc, c]
+    start(grads_ref, mine, send_g.at[0], came, z_pair, x)
+    start(grads_ref, mine, send_g.at[1], came, z, ox * 2 + c)
+    start(grads_ref, mine, send_g.at[2], came, z_pair, ox * 2 + c)
+    start(grads_ref, mine, send_g.at[3], came, z, xc * 2 + oc)
+
+    def hash_rows(low, high):
+        @pl.loop(low, high)
+        def _(i):
+            h = i // (half // 16)
+            r = i % (half // 16)
+            first = ((z + 2 * h) % 4) * feat_rows + x * half + r * 16
+            feat_term = (first + lax.broadcasted_iota(jnp.int32, (16, 128), 0)) * 97001
+            for j in range(2 * width // 128):
+                signs[h, pl.ds(pl.multiple_of(r * 16, 16), 16), pl.ds(j * 128, 128)] = sign_tile(
+                    coord_term[:, pl.ds(j * 128, 128)], feat_term
+                )
+
+    def arrived(a, b, k):
+        slot = grads.at[a, b, k]
+        remote(slot, slot, send_g.at[0], recv_g.at[a, b, k], z_pair, x).wait_recv()
+
+    def forward(a, b, n):
+        arrived(a, b, c)
+        slot = grads.at[a, b, c]
+        start(slot, slot, send_g.at[n], recv_g.at[a, b, c], z, xc * 2 + oc)
+
+    def sums(b, h):
+        total = None
+        for a in range(2):
+            one = lax.dot_general(
+                grads[a, b].reshape(2 * n_ex, width), signs[h, :, pl.ds(a * width, width)],
+                (((1,), (1,)), ((), ())), preferred_element_type=jnp.float32,
+            )
+            total = one if total is None else total + one
+        return total
+
+    steps = half // 16
+    hash_rows(0, steps)
+    forward(oz, xc, 4)
+    hash_rows(steps, 2 * steps)
+    forward(zz, ox, 5)
+    for n, b in enumerate((xc, ox)):
+        if n == 0:
+            arrived(zz, xc, oc)
+            arrived(oz, xc, oc)
+        else:
+            forward(oz, ox, 6)
+            arrived(zz, ox, oc)
+            arrived(oz, ox, oc)
+        part[n] = sums(b, 1).astype(jnp.bfloat16)
+        start(part.at[n], part_in.at[n], send_p.at[n], recv_p.at[n], z_far, x)
+        own[n] = sums(b, 0)
+
+    for n, b in enumerate((xc, ox)):
+        remote(part.at[n], part_in.at[n], send_p.at[n], recv_p.at[n], z_far, x).wait_recv()
+        done = (own[n] + part_in[n].astype(jnp.float32)) / math.sqrt(4 * width)
+        feat[b] = done.astype(jnp.bfloat16).reshape(2, n_ex, half)
+        for k in (oc,) if n == 0 else (c, oc):
+            t = b * 2 + k
+            slot = 0 if n == 0 else (1 if k is c else 2)
+            start(feat.at[b, k], feat_in.at[x], send_f.at[slot], recv_f.at[x], z, t)
+    feat_in[x] = feat[xc, c]
+
+    everyone = feat[...].reshape(4 * n_ex, half)
+    for t in range(4):
+        block = lax.dot_general(
+            everyone, feat[t // 2, t % 2], (((1,), (1,)), ((), ())), preferred_element_type=jnp.float32
+        ) / FEATS
+        for row in range(4):
+            gram[row * 4 + t] = block[row * n_ex:(row + 1) * n_ex].astype(jnp.bfloat16)
+    for d in range(1, 16):
+        t = (me + d) % 16
+        start(gram.at[t], gram_in.at[me], send_k.at[d], recv_k.at[me], t // 4, t % 4)
+
+    for d in range(4):
+        t = (x + d) % 4
+        if d:
+            remote(feat_in.at[t], feat_in.at[t], send_f.at[0], recv_f.at[t], z, t).wait_recv()
+        feats_ref[pl.ds(pl.multiple_of(t * half, half), half), :] = feat_in[t].T
+
+    total = gram[me].astype(jnp.float32)
+    for d in range(1, 16):
+        t = (me + d) % 16
+        remote(gram_in.at[t], gram_in.at[t], send_k.at[0], recv_k.at[t], t // 4, t % 4).wait_recv()
+        total = total + gram_in[t].astype(jnp.float32)
+    kern_ref[...] = total
+    for copy in sends:
+        copy.wait_send()
+
+
+def fused(gradients, hash_salt, slab_offset):
+    n_ex, width = gradients.shape
+    half = FEATS // 16
+    dma = pltpu.SemaphoreType.DMA
+    return pl.pallas_call(
+        fused_kernel,
+        out_shape=(
+            jax.ShapeDtypeStruct((FEATS // 4, n_ex), jnp.bfloat16),
+            jax.ShapeDtypeStruct((n_ex, n_ex), jnp.float32),
+        ),
+        in_specs=[pl.BlockSpec(memory_space=pltpu.SMEM)] * 2 + [pl.BlockSpec(memory_space=pltpu.VMEM)],
+        out_specs=(pl.BlockSpec(memory_space=pltpu.VMEM),) * 2,
+        scratch_shapes=[
+            pltpu.VMEM((2, 2, 2, n_ex, width), jnp.bfloat16),
+            pltpu.VMEM((2, half, 2 * width), jnp.bfloat16),
+            pltpu.VMEM((16, 2 * width), jnp.int32),
+            pltpu.VMEM((2, 2 * n_ex, half), jnp.bfloat16),
+            pltpu.VMEM((2, 2 * n_ex, half), jnp.bfloat16),
+            pltpu.VMEM((2, 2 * n_ex, half), jnp.float32),
+            pltpu.VMEM((2, 2, n_ex, half), jnp.bfloat16),
+            pltpu.VMEM((4, n_ex, half), jnp.bfloat16),
+            pltpu.VMEM((16, n_ex, n_ex), jnp.bfloat16),
+            pltpu.VMEM((16, n_ex, n_ex), jnp.bfloat16),
+            dma((7,)), dma((2, 2, 2)),
+            dma((2,)), dma((2,)),
+            dma((3,)), dma((4,)),
+            dma((16,)), dma((16,)),
+        ],
+        compiler_params=pltpu.CompilerParams(
+            collective_id=0, has_side_effects=True, vmem_limit_bytes=48 * 2**20
+        ),
+    )(hash_salt, slab_offset, gradients)
+
+
 def solution(mesh):
+    small = mesh.shape["coord"] == 4 and mesh.shape["ex"] == 4
     return jax.shard_map(
-        general,
+        fused if small else general,
         mesh=mesh,
         in_specs=(P(("groups", "ex"), "coord"), P("groups"), P("groups")),
         out_specs=(P("coord", ("groups", "ex")), P(("groups", "coord"), "ex")),

time: 128 us -> 52.9 us (0.41)
  blocking collectives: 41.8 us -> 0 us
  waiting for transfers between devices: 40.5 us -> 0 us
  Pallas kernels: 13.6 us -> 48.2 us
  between operations: 15.4 us -> 1.94 us
  starting transfers between devices: 10.3 us -> 0 us
  local copies, waits for them, and re-layouts: 4.59 us -> 2.56 us
    all_to_all x1 -> x0, blocking collectives: 41.8 us -> none  [general(): lax.all_to_all(part.reshape(coord_parts, sub, examples), 'coord', 0, 0)]
    pallas_call x1, Pallas kernels: 13.6 us -> 48.2 us  [fused(): pl.pallas_call(fused_kernel, out_shape=(jax.ShapeDtypeStruct((FEATS // 4,...]
    all_gather x1 -> x0, waiting for transfers between devices: 22.8 us -> none  [general(): gathered = lax.all_gather(gradients, 'ex', axis=0, tiled=True)]
    all_to_all x3 -> x0, waiting for transfers between devices: 17 us -> none  [the longest x1 6.6 us: general(): features = lax.all_to_all(blocks, 'ex', 0, 0).reshape(feat_rows, ex_local)]
    all_to_all x3 -> x0, starting transfers between devices: 10.2 us -> none  [the longest x1 3.46 us: general(): features = lax.all_to_all(blocks, 'ex', 0, 0).reshape(feat_rows, ex_local)]
    reshape x3 -> x0, local copies, waits for them, and re-layouts: 1.53 us -> none  [the longest x1 0.79 us: general(): features = lax.all_to_all(blocks, 'ex', 0, 0).reshape(feat_rows, ex_local)]
  transfers between devices with their start and end apart: 4 -> 0, of which waited for: 4 -> 0; matrix products, arithmetic and copies ran while one was open for 2% -> 0% of each run, Pallas kernels for 0% -> 0%
where the time goes in v2:
time: 52.9 us; the launch traced here: 52.7 us
  Pallas kernels  48.2 us (91%)
  local copies, waits for them, and re-layouts  2.56 us (5%)
  between operations  1.94 us (4%)
    pallas_call x1, Pallas kernels, fused(): pl.pallas_call(fused_kernel, out_shape=(jax.ShapeDtypeStruct((FEATS // 4,...  48.2 us
    unnamed x3, local copies, waits for them, and re-layouts  1.61 us

profile of v2, /device:TPU:0, one launch (start us, length us, event | category | flops | bytes accessed | tf_op | source)
XLA Modules:
  0.0 52.7 jit_solution(10282250218809087151)
XLA Ops:
  1.9 0.0 copy-start
  1.9 1.0 %copy-done = bf16[96,2048]{1,0:T(8,128)(2,1)S(1)} copy-done((bf16[96,2048]{1,0:T(8,128)(2,1)S(1)}, bf16[96,2048]{1,0:T(8,128)(2,1)}, u32[]{:S(2)}) %copy-start) | copy-done | bytes 393240
  2.9 48.2 %shard_map.50 = (bf16[2048,96]{1,0:T(8,128)(2,1)S(1)}, f32[96,96]{1,0:T(8,128)S(1)}) custom-call(s32[1]{0:T(128)S(6)} %copy.7.salt_ref, s32[1]{0:T(128)S(6)} %copy.8.offset_ref, bf16[96,2048]{1,0:T(8,128)(2,1)S(1)} %copy-done), custom_call_target="tpu_custom_call" | custom-call | tf_op jit(solution)/shard_map/pallas_call | solution.py:228
  51.1 1.0 %copy.5 = bf16[2048,96]{0,1:T(8,128)(2,1)} copy(bf16[2048,96]{1,0:T(8,128)(2,1)S(1)} %get-tuple-element.2) | data formatting | bytes 786432 | tf_op jit(solution)/shard_map/pallas_call | solution.py:228
  52.1 0.6 %copy.9 = f32[96,96]{1,0:T(8,128)} copy(f32[96,96]{1,0:T(8,128)S(1)} %get-tuple-element.7) | data formatting | bytes 73728
Async XLA Ops:
  1.9 1.0 %copy-start = (bf16[96,2048]{1,0:T(8,128)(2,1)S(1)}, bf16[96,2048]{1,0:T(8,128)(2,1)}, u32[]{:S(2)}) copy-start(bf16[96,2048]{1,0:T(8,128)(2,1)} %grads_ref.1) | copy-start | bytes 1179652

commit v3 on v2

--- a/solution.py
+++ b/solution.py
@@ -92,8 +92,8 @@
 
 def fused_kernel(
     salt_ref, offset_ref, grads_ref, feats_ref, kern_ref,
-    grads, signs, coord_term, part, part_in, own, feat, feat_in, gram, gram_in,
-    send_g, recv_g, send_p, recv_p, send_f, recv_f, send_k, recv_k,
+    grads, signs, coord_term, part, part_in, own, feat, feat_in, gram, gram_sib, gram_out, gram_in,
+    local, send_g, recv_g, send_p, recv_p, send_f, recv_f, send_s, recv_s, send_k, recv_k,
 ):
     z, x = lax.axis_index("coord"), lax.axis_index("ex")
     xc, c = x // 2, x % 2
@@ -103,6 +103,7 @@
     ox = 1 - xc
     me = z * 4 + x
     n_ex, width = grads_ref.shape
+    cut = n_ex // 2
     half = signs.shape[1]
     feat_rows = FEATS // 4
     sends = []
@@ -126,15 +127,19 @@
         )
     ids = offset_ref[0] + (z // 2) * (2 * width) + lax.broadcasted_iota(jnp.int32, (16, 2 * width), 1)
     coord_term[...] = (ids * 2654435) ^ salt_ref[0]
-    grads[zz, xc, c] = grads_ref[...]
     pl.semaphore_wait(barrier, 15)
 
-    mine = grads.at[zz, xc, c]
-    came = recv_g.at[zz, xc, c]
-    start(grads_ref, mine, send_g.at[0], came, z_pair, x)
-    start(grads_ref, mine, send_g.at[1], came, z, ox * 2 + c)
-    start(grads_ref, mine, send_g.at[2], came, z_pair, ox * 2 + c)
-    start(grads_ref, mine, send_g.at[3], came, z, xc * 2 + oc)
+    copies = []
+    for n, (zt, xt, cuts) in enumerate(((z_pair, x, (0, 1)), (z, ox * 2 + c, (1, 0)), (z, xc * 2 + oc, (0, 1)))):
+        for k in cuts:
+            start(
+                grads_ref.at[pl.ds(k * cut, cut)], grads.at[zz, xc, k, c],
+                send_g.at[2 * n + k], recv_g.at[zz, xc, k, c], zt, xt,
+            )
+    for k in range(2):
+        copy = pltpu.make_async_copy(grads_ref.at[pl.ds(k * cut, cut)], grads.at[zz, xc, k, c], local.at[k])
+        copy.start()
+        copies.append(copy)
 
     def hash_rows(low, high):
         @pl.loop(low, high)
@@ -148,73 +153,113 @@
                     coord_term[:, pl.ds(j * 128, 128)], feat_term
                 )
 
-    def arrived(a, b, k):
-        slot = grads.at[a, b, k]
-        remote(slot, slot, send_g.at[0], recv_g.at[a, b, k], z_pair, x).wait_recv()
-
-    def forward(a, b, n):
-        arrived(a, b, c)
-        slot = grads.at[a, b, c]
-        start(slot, slot, send_g.at[n], recv_g.at[a, b, c], z, xc * 2 + oc)
-
-    def sums(b, h):
+    def arrived(a, b, k, core):
+        slot = grads.at[a, b, k, core]
+        remote(slot, slot, send_g.at[0], recv_g.at[a, b, k, core], z_pair, x).wait_recv()
+
+    def pass_on(a, b, k, n, zt, xt):
+        slot = grads.at[a, b, k, c]
+        start(slot, slot, send_g.at[n], recv_g.at[a, b, k, c], zt, xt)
+
+    def forward(a, b, k, n):
+        pass_on(a, b, k, n, z, xc * 2 + oc)
+
+    def sums(b, k, h):
         total = None
         for a in range(2):
             one = lax.dot_general(
-                grads[a, b].reshape(2 * n_ex, width), signs[h, :, pl.ds(a * width, width)],
+                grads[a, b, k].reshape(n_ex, width), signs[h, :, pl.ds(a * width, width)],
                 (((1,), (1,)), ((), ())), preferred_element_type=jnp.float32,
             )
             total = one if total is None else total + one
         return total
 
+    def exchange(n):
+        return remote(part.at[n], part_in.at[n], send_p.at[n], recv_p.at[n], z_far, x)
+
+    def give(n, b, k):
+        arrived(zz, b, k, oc)
+        arrived(oz, b, k, oc)
+        part[n] = sums(b, k, 1).astype(jnp.bfloat16)
+        copy = exchange(n)
+        copy.start()
+        sends.append(copy)
+
     steps = half // 16
-    hash_rows(0, steps)
-    forward(oz, xc, 4)
     hash_rows(steps, 2 * steps)
-    forward(zz, ox, 5)
-    for n, b in enumerate((xc, ox)):
-        if n == 0:
-            arrived(zz, xc, oc)
-            arrived(oz, xc, oc)
-        else:
-            forward(oz, ox, 6)
-            arrived(zz, ox, oc)
-            arrived(oz, ox, oc)
-        part[n] = sums(b, 1).astype(jnp.bfloat16)
-        start(part.at[n], part_in.at[n], send_p.at[n], recv_p.at[n], z_far, x)
-        own[n] = sums(b, 0)
-
-    for n, b in enumerate((xc, ox)):
-        remote(part.at[n], part_in.at[n], send_p.at[n], recv_p.at[n], z_far, x).wait_recv()
+    for copy in copies:
+        copy.wait()
+    arrived(oz, xc, 0, c)
+    pass_on(oz, xc, 0, 6, z, ox * 2 + c)
+    forward(oz, xc, 0, 8)
+    arrived(zz, ox, 1, c)
+    pass_on(zz, ox, 1, 7, z_pair, x)
+    forward(zz, ox, 1, 9)
+    give(0, xc, 0)
+    hash_rows(0, steps // 2)
+    arrived(oz, xc, 1, c)
+    forward(oz, xc, 1, 10)
+    give(1, xc, 1)
+    arrived(zz, ox, 0, c)
+    forward(zz, ox, 0, 11)
+    hash_rows(steps // 2, steps)
+    arrived(oz, ox, 0, c)
+    forward(oz, ox, 0, 12)
+    give(2, ox, 0)
+    arrived(oz, ox, 1, c)
+    forward(oz, ox, 1, 13)
+    give(3, ox, 1)
+    chunks = ((xc, 0), (xc, 1), (ox, 0), (ox, 1))
+    for n, (b, k) in enumerate(chunks):
+        own[n] = sums(b, k, 0)
+
+    for n, (b, k) in enumerate(chunks):
+        exchange(n).wait_recv()
         done = (own[n] + part_in[n].astype(jnp.float32)) / math.sqrt(4 * width)
-        feat[b] = done.astype(jnp.bfloat16).reshape(2, n_ex, half)
-        for k in (oc,) if n == 0 else (c, oc):
-            t = b * 2 + k
-            slot = 0 if n == 0 else (1 if k is c else 2)
-            start(feat.at[b, k], feat_in.at[x], send_f.at[slot], recv_f.at[x], z, t)
+        feat[b, :, pl.ds(k * cut, cut)] = done.astype(jnp.bfloat16).reshape(2, cut, half)
+        if n == 1:
+            start(feat.at[xc, oc], feat_in.at[x], send_f.at[0], recv_f.at[x], z, xc * 2 + oc)
+        if n == 3:
+            start(feat.at[ox, c], feat_in.at[x], send_f.at[1], recv_f.at[x], z, ox * 2 + c)
+            start(feat.at[ox, oc], feat_in.at[x], send_f.at[2], recv_f.at[x], z, ox * 2 + oc)
+
+    everyone = feat[...].reshape(4 * n_ex, half)
+
+    def blocks(core):
+        for b in range(2):
+            block = lax.dot_general(
+                everyone, feat[b, core], (((1,), (1,)), ((), ())), preferred_element_type=jnp.float32
+            ) / FEATS
+            for row in range(4):
+                gram[core, row * 2 + b] = block[row * n_ex:(row + 1) * n_ex].astype(jnp.bfloat16)
+
+    chip = z * 2 + xc
+    blocks(oc)
+    sibling = remote(gram.at[oc], gram_sib, send_s, recv_s, z, xc * 2 + oc)
+    sibling.start()
+    sends.append(sibling)
+    blocks(c)
     feat_in[x] = feat[xc, c]
-
-    everyone = feat[...].reshape(4 * n_ex, half)
-    for t in range(4):
-        block = lax.dot_general(
-            everyone, feat[t // 2, t % 2], (((1,), (1,)), ((), ())), preferred_element_type=jnp.float32
-        ) / FEATS
-        for row in range(4):
-            gram[row * 4 + t] = block[row * n_ex:(row + 1) * n_ex].astype(jnp.bfloat16)
-    for d in range(1, 16):
-        t = (me + d) % 16
-        start(gram.at[t], gram_in.at[me], send_k.at[d], recv_k.at[me], t // 4, t % 4)
+    sibling.wait_recv()
+    gram_out[...] = (gram[c].astype(jnp.float32) + gram_sib[...].astype(jnp.float32)).astype(jnp.bfloat16)
+    for d in range(1, 8):
+        t = (chip + d) % 8
+        start(
+            gram_out.at[t], gram_in.at[chip], send_k.at[d], recv_k.at[chip], t // 2, (t % 2) * 2 + c
+        )
 
     for d in range(4):
         t = (x + d) % 4
         if d:
             remote(feat_in.at[t], feat_in.at[t], send_f.at[0], recv_f.at[t], z, t).wait_recv()
-        feats_ref[pl.ds(pl.multiple_of(t * half, half), half), :] = feat_in[t].T
-
-    total = gram[me].astype(jnp.float32)
-    for d in range(1, 16):
-        t = (me + d) % 16
-        remote(gram_in.at[t], gram_in.at[t], send_k.at[0], recv_k.at[t], t // 4, t % 4).wait_recv()
+        feats_ref[:, pl.ds(pl.multiple_of(t * half, half), half)] = feat_in[t]
+
+    total = gram[c, chip].astype(jnp.float32) + gram_sib[chip].astype(jnp.float32)
+    for d in range(1, 8):
+        t = (chip + d) % 8
+        remote(
+            gram_in.at[t], gram_in.at[t], send_k.at[0], recv_k.at[t], t // 2, (t % 2) * 2 + c
+        ).wait_recv()
         total = total + gram_in[t].astype(jnp.float32)
     kern_ref[...] = total
     for copy in sends:
@@ -225,34 +270,38 @@
     n_ex, width = gradients.shape
     half = FEATS // 16
     dma = pltpu.SemaphoreType.DMA
-    return pl.pallas_call(
+    flipped, kernel = pl.pallas_call(
         fused_kernel,
         out_shape=(
-            jax.ShapeDtypeStruct((FEATS // 4, n_ex), jnp.bfloat16),
+            jax.ShapeDtypeStruct((n_ex, FEATS // 4), jnp.bfloat16),
             jax.ShapeDtypeStruct((n_ex, n_ex), jnp.float32),
         ),
-        in_specs=[pl.BlockSpec(memory_space=pltpu.SMEM)] * 2 + [pl.BlockSpec(memory_space=pltpu.VMEM)],
+        in_specs=[pl.BlockSpec(memory_space=pltpu.SMEM)] * 2 + [pl.BlockSpec(memory_space=pltpu.HBM)],
         out_specs=(pl.BlockSpec(memory_space=pltpu.VMEM),) * 2,
         scratch_shapes=[
-            pltpu.VMEM((2, 2, 2, n_ex, width), jnp.bfloat16),
+            pltpu.VMEM((2, 2, 2, 2, n_ex // 2, width), jnp.bfloat16),
             pltpu.VMEM((2, half, 2 * width), jnp.bfloat16),
             pltpu.VMEM((16, 2 * width), jnp.int32),
-            pltpu.VMEM((2, 2 * n_ex, half), jnp.bfloat16),
-            pltpu.VMEM((2, 2 * n_ex, half), jnp.bfloat16),
-            pltpu.VMEM((2, 2 * n_ex, half), jnp.float32),
+            pltpu.VMEM((4, n_ex, half), jnp.bfloat16),
+            pltpu.VMEM((4, n_ex, half), jnp.bfloat16),
+            pltpu.VMEM((4, n_ex, half), jnp.float32),
             pltpu.VMEM((2, 2, n_ex, half), jnp.bfloat16),
             pltpu.VMEM((4, n_ex, half), jnp.bfloat16),
-            pltpu.VMEM((16, n_ex, n_ex), jnp.bfloat16),
-            pltpu.VMEM((16, n_ex, n_ex), jnp.bfloat16),
-            dma((7,)), dma((2, 2, 2)),
-            dma((2,)), dma((2,)),
+            pltpu.VMEM((2, 8, n_ex, n_ex), jnp.bfloat16),
+            pltpu.VMEM((8, n_ex, n_ex), jnp.bfloat16),
+            pltpu.VMEM((8, n_ex, n_ex), jnp.bfloat16),
+            pltpu.VMEM((8, n_ex, n_ex), jnp.bfloat16),
+            dma((2,)), dma((14,)), dma((2, 2, 2, 2)),
+            dma((4,)), dma((4,)),
             dma((3,)), dma((4,)),
-            dma((16,)), dma((16,)),
+            dma, dma,
+            dma((8,)), dma((8,)),
         ],
         compiler_params=pltpu.CompilerParams(
             collective_id=0, has_side_effects=True, vmem_limit_bytes=48 * 2**20
         ),
     )(hash_salt, slab_offset, gradients)
+    return flipped.T, kernel
 
 
 def solution(mesh):

time: 52.9 us -> 47.1 us (0.89)
  Pallas kernels: 48.2 us -> 42.6 us
    pallas_call x1, Pallas kernels: 48.2 us -> 42.6 us  [fused(): pl.pallas_call(fused_kernel, out_shape=(jax.ShapeDtypeStruct((n_ex, FEATS...]
    pallas_call x1 -> x0, local copies, waits for them, and re-layouts: 0.95 us -> none  [fused(): pl.pallas_call(fused_kernel, out_shape=(jax.ShapeDtypeStruct((FEATS // 4,...]
    unnamed x3 -> x4, local copies, waits for them, and re-layouts: 1.61 us -> 2.36 us
where the time goes in v3:
time: 47.1 us; the launch traced here: 46.9 us
  Pallas kernels  42.6 us (90%)
  local copies, waits for them, and re-layouts  2.36 us (5%)
  between operations  1.94 us (4%)
    pallas_call x1, Pallas kernels, fused(): pl.pallas_call(fused_kernel, out_shape=(jax.ShapeDtypeStruct((n_ex, FEATS...  42.6 us
    unnamed x4, local copies, waits for them, and re-layouts  2.36 us

profile of v3, /device:TPU:0, one launch (start us, length us, event | category | flops | bytes accessed | tf_op | source)
XLA Modules:
  0.0 46.9 jit_solution(3101127170557349433)
XLA Ops:
  1.9 0.0 copy-start
  1.9 1.0 %copy-done = bf16[96,2048]{1,0:T(8,128)(2,1)S(1)} copy-done((bf16[96,2048]{1,0:T(8,128)(2,1)S(1)}, bf16[96,2048]{1,0:T(8,128)(2,1)}, u32[]{:S(2)}) %copy-start) | copy-done | bytes 393240
  2.9 42.6 %shard_map.50 = (bf16[96,2048]{1,0:T(8,128)(2,1)S(1)}, f32[96,96]{1,0:T(8,128)S(1)}) custom-call(s32[1]{0:T(128)S(6)} %copy.7.salt_ref, s32[1]{0:T(128)S(6)} %copy.8.offset_ref, bf16[96,2048]{1,0:T(8,128)(2,1)S(1)} %copy-done), custom_call_target="tpu_custom_call" | custom-call | tf_op jit(solution)/shard_map/pallas_call | solution.py:273
  45.5 0.7 %copy.9 = bf16[2048,96]{0,1:T(8,128)(2,1)} copy(bf16[2048,96]{0,1:T(8,128)(2,1)S(1)} %bitcast.1) | data formatting | bytes 786432
  46.3 0.6 %copy.10 = f32[96,96]{1,0:T(8,128)} copy(f32[96,96]{1,0:T(8,128)S(1)} %get-tuple-element.9) | data formatting | bytes 73728
Async XLA Ops:
  1.9 1.0 %copy-start = (bf16[96,2048]{1,0:T(8,128)(2,1)S(1)}, bf16[96,2048]{1,0:T(8,128)(2,1)}, u32[]{:S(2)}) copy-start(bf16[96,2048]{1,0:T(8,128)(2,1)} %grads_ref.1) | copy-start | bytes 1179652

commit v4 on v3

--- a/solution.py
+++ b/solution.py
@@ -130,7 +130,7 @@
     pl.semaphore_wait(barrier, 15)
 
     copies = []
-    for n, (zt, xt, cuts) in enumerate(((z_pair, x, (0, 1)), (z, ox * 2 + c, (1, 0)), (z, xc * 2 + oc, (0, 1)))):
+    for n, (zt, xt, cuts) in enumerate(((z_pair, x, (0, 1)), (z, ox * 2 + c, (0, 1)), (z, xc * 2 + oc, (0, 1)))):
         for k in cuts:
             start(
                 grads_ref.at[pl.ds(k * cut, cut)], grads.at[zz, xc, k, c],
@@ -192,16 +192,16 @@
     arrived(oz, xc, 0, c)
     pass_on(oz, xc, 0, 6, z, ox * 2 + c)
     forward(oz, xc, 0, 8)
-    arrived(zz, ox, 1, c)
-    pass_on(zz, ox, 1, 7, z_pair, x)
-    forward(zz, ox, 1, 9)
     give(0, xc, 0)
     hash_rows(0, steps // 2)
     arrived(oz, xc, 1, c)
+    pass_on(oz, xc, 1, 7, z, ox * 2 + c)
     forward(oz, xc, 1, 10)
     give(1, xc, 1)
     arrived(zz, ox, 0, c)
     forward(zz, ox, 0, 11)
+    arrived(zz, ox, 1, c)
+    forward(zz, ox, 1, 9)
     hash_rows(steps // 2, steps)
     arrived(oz, ox, 0, c)
     forward(oz, ox, 0, 12)

time: 47.1 us -> 46.4 us (0.985)
  Pallas kernels: 42.6 us -> 42 us
    pallas_call x1, Pallas kernels: 42.6 us -> 42 us  [fused(): pl.pallas_call(fused_kernel, out_shape=(jax.ShapeDtypeStruct((n_ex, FEATS...]
where the time goes in v4:
time: 46.4 us; the launch traced here: 46.3 us
  Pallas kernels  42 us (91%)
  local copies, waits for them, and re-layouts  2.36 us (5%)
  between operations  1.94 us (4%)
    pallas_call x1, Pallas kernels, fused(): pl.pallas_call(fused_kernel, out_shape=(jax.ShapeDtypeStruct((n_ex, FEATS...  42 us
    unnamed x4, local copies, waits for them, and re-layouts  2.36 us

profile of v4, /device:TPU:0, one launch (start us, length us, event | category | flops | bytes accessed | tf_op | source)
XLA Modules:
  0.0 46.3 jit_solution(10320447537266042716)
XLA Ops:
  1.9 0.0 copy-start
  1.9 1.0 %copy-done = bf16[96,2048]{1,0:T(8,128)(2,1)S(1)} copy-done((bf16[96,2048]{1,0:T(8,128)(2,1)S(1)}, bf16[96,2048]{1,0:T(8,128)(2,1)}, u32[]{:S(2)}) %copy-start) | copy-done | bytes 393240
  2.9 42.0 %shard_map.50 = (bf16[96,2048]{1,0:T(8,128)(2,1)S(1)}, f32[96,96]{1,0:T(8,128)S(1)}) custom-call(s32[1]{0:T(128)S(6)} %copy.7.salt_ref, s32[1]{0:T(128)S(6)} %copy.8.offset_ref, bf16[96,2048]{1,0:T(8,128)(2,1)S(1)} %copy-done), custom_call_target="tpu_custom_call" | custom-call | tf_op jit(solution)/shard_map/pallas_call | solution.py:273
  44.9 0.7 %copy.9 = bf16[2048,96]{0,1:T(8,128)(2,1)} copy(bf16[2048,96]{0,1:T(8,128)(2,1)S(1)} %bitcast.1) | data formatting | bytes 786432
  45.6 0.6 %copy.10 = f32[96,96]{1,0:T(8,128)} copy(f32[96,96]{1,0:T(8,128)S(1)} %get-tuple-element.9) | data formatting | bytes 73728
Async XLA Ops:
  1.9 1.0 %copy-start = (bf16[96,2048]{1,0:T(8,128)(2,1)S(1)}, bf16[96,2048]{1,0:T(8,128)(2,1)}, u32[]{:S(2)}) copy-start(bf16[96,2048]{1,0:T(8,128)(2,1)} %grads_ref.1) | copy-start | bytes 1179652

commit v5 on v4

--- a/solution.py
+++ b/solution.py
@@ -101,7 +101,6 @@
     z_pair, z_far = z + 1 - 2 * zz, (z + 2) % 4
     oc, oz = 1 - c, 1 - zz
     ox = 1 - xc
-    me = z * 4 + x
     n_ex, width = grads_ref.shape
     cut = n_ex // 2
     half = signs.shape[1]
@@ -120,14 +119,18 @@
         sends.append(copy)
 
     barrier = pltpu.get_barrier_semaphore()
-    for d in range(1, 16):
-        t = (me + d) % 16
+    chip = z * 2 + xc
+    greeted = [(z, xc * 2 + oc), (z, ox * 2 + oc)]
+    for d in range(1, 8):
+        t = (chip + d) % 8
+        greeted.append((t // 2, (t % 2) * 2 + c))
+    for zt, xt in greeted:
         pl.semaphore_signal(
-            barrier, inc=1, device_id={"coord": t // 4, "ex": t % 4}, device_id_type=pl.DeviceIdType.MESH
+            barrier, inc=1, device_id={"coord": zt, "ex": xt}, device_id_type=pl.DeviceIdType.MESH
         )
     ids = offset_ref[0] + (z // 2) * (2 * width) + lax.broadcasted_iota(jnp.int32, (16, 2 * width), 1)
     coord_term[...] = (ids * 2654435) ^ salt_ref[0]
-    pl.semaphore_wait(barrier, 15)
+    pl.semaphore_wait(barrier, 9)
 
     copies = []
     for n, (zt, xt, cuts) in enumerate(((z_pair, x, (0, 1)), (z, ox * 2 + c, (0, 1)), (z, xc * 2 + oc, (0, 1)))):
@@ -203,25 +206,29 @@
     arrived(zz, ox, 1, c)
     forward(zz, ox, 1, 9)
     hash_rows(steps // 2, steps)
+    own[0] = sums(xc, 0, 0)
+    own[1] = sums(xc, 1, 0)
     arrived(oz, ox, 0, c)
     forward(oz, ox, 0, 12)
     give(2, ox, 0)
+    own[2] = sums(ox, 0, 0)
     arrived(oz, ox, 1, c)
     forward(oz, ox, 1, 13)
     give(3, ox, 1)
     chunks = ((xc, 0), (xc, 1), (ox, 0), (ox, 1))
-    for n, (b, k) in enumerate(chunks):
-        own[n] = sums(b, k, 0)
+    own[3] = sums(ox, 1, 0)
 
     for n, (b, k) in enumerate(chunks):
         exchange(n).wait_recv()
         done = (own[n] + part_in[n].astype(jnp.float32)) / math.sqrt(4 * width)
         feat[b, :, pl.ds(k * cut, cut)] = done.astype(jnp.bfloat16).reshape(2, cut, half)
-        if n == 1:
-            start(feat.at[xc, oc], feat_in.at[x], send_f.at[0], recv_f.at[x], z, xc * 2 + oc)
-        if n == 3:
-            start(feat.at[ox, c], feat_in.at[x], send_f.at[1], recv_f.at[x], z, ox * 2 + c)
-            start(feat.at[ox, oc], feat_in.at[x], send_f.at[2], recv_f.at[x], z, ox * 2 + oc)
+        rows = pl.ds(k * cut, cut)
+        into = feat_in.at[x, rows]
+        if n < 2:
+            start(feat.at[xc, oc, rows], into, send_f.at[0, k], recv_f.at[x, k], z, xc * 2 + oc)
+        else:
+            start(feat.at[ox, c, rows], into, send_f.at[1, k], recv_f.at[x, k], z, ox * 2 + c)
+            start(feat.at[ox, oc, rows], into, send_f.at[2, k], recv_f.at[x, k], z, ox * 2 + oc)
 
     everyone = feat[...].reshape(4 * n_ex, half)
 
@@ -233,7 +240,6 @@
             for row in range(4):
                 gram[core, row * 2 + b] = block[row * n_ex:(row + 1) * n_ex].astype(jnp.bfloat16)
 
-    chip = z * 2 + xc
     blocks(oc)
     sibling = remote(gram.at[oc], gram_sib, send_s, recv_s, z, xc * 2 + oc)
     sibling.start()
@@ -251,7 +257,9 @@
     for d in range(4):
         t = (x + d) % 4
         if d:
-            remote(feat_in.at[t], feat_in.at[t], send_f.at[0], recv_f.at[t], z, t).wait_recv()
+            for k in range(2):
+                slot = feat_in.at[t, pl.ds(k * cut, cut)]
+                remote(slot, slot, send_f.at[0, k], recv_f.at[t, k], z, t).wait_recv()
         feats_ref[:, pl.ds(pl.multiple_of(t * half, half), half)] = feat_in[t]
 
     total = gram[c, chip].astype(jnp.float32) + gram_sib[chip].astype(jnp.float32)
@@ -293,7 +301,7 @@
             pltpu.VMEM((8, n_ex, n_ex), jnp.bfloat16),
             dma((2,)), dma((14,)), dma((2, 2, 2, 2)),
             dma((4,)), dma((4,)),
-            dma((3,)), dma((4,)),
+            dma((3, 2)), dma((4, 2)),
             dma, dma,
             dma((8,)), dma((8,)),
         ],

time: 46.4 us -> 47.9 us (1.032)
  Pallas kernels: 42 us -> 43.5 us
    pallas_call x1, Pallas kernels: 42 us -> 43.5 us  [fused(): pl.pallas_call(fused_kernel, out_shape=(jax.ShapeDtypeStruct((n_ex, FEATS...]
where the time goes in v5:
time: 47.9 us; the launch traced here: 47.8 us
  Pallas kernels  43.5 us (91%)
  local copies, waits for them, and re-layouts  2.36 us (5%)
  between operations  1.94 us (4%)
    pallas_call x1, Pallas kernels, fused(): pl.pallas_call(fused_kernel, out_shape=(jax.ShapeDtypeStruct((n_ex, FEATS...  43.5 us
    unnamed x4, local copies, waits for them, and re-layouts  2.36 us

profile of v5, /device:TPU:0, one launch (start us, length us, event | category | flops | bytes accessed | tf_op | source)
XLA Modules:
  0.0 47.8 jit_solution(6546559914915201754)
XLA Ops:
  1.9 0.0 copy-start
  1.9 1.0 %copy-done = bf16[96,2048]{1,0:T(8,128)(2,1)S(1)} copy-done((bf16[96,2048]{1,0:T(8,128)(2,1)S(1)}, bf16[96,2048]{1,0:T(8,128)(2,1)}, u32[]{:S(2)}) %copy-start) | copy-done | bytes 393240
  2.9 43.5 %shard_map.50 = (bf16[96,2048]{1,0:T(8,128)(2,1)S(1)}, f32[96,96]{1,0:T(8,128)S(1)}) custom-call(s32[1]{0:T(128)S(6)} %copy.7.salt_ref, s32[1]{0:T(128)S(6)} %copy.8.offset_ref, bf16[96,2048]{1,0:T(8,128)(2,1)S(1)} %copy-done), custom_call_target="tpu_custom_call" | custom-call | tf_op jit(solution)/shard_map/pallas_call | solution.py:281
  46.4 0.7 %copy.9 = bf16[2048,96]{0,1:T(8,128)(2,1)} copy(bf16[2048,96]{0,1:T(8,128)(2,1)S(1)} %bitcast.1) | data formatting | bytes 786432
  47.2 0.6 %copy.10 = f32[96,96]{1,0:T(8,128)} copy(f32[96,96]{1,0:T(8,128)S(1)} %get-tuple-element.9) | data formatting | bytes 73728
Async XLA Ops:
  1.9 1.0 %copy-start = (bf16[96,2048]{1,0:T(8,128)(2,1)S(1)}, bf16[96,2048]{1,0:T(8,128)(2,1)}, u32[]{:S(2)}) copy-start(bf16[96,2048]{1,0:T(8,128)(2,1)} %grads_ref.1) | copy-start | bytes 1179652

commit v6 on v5

--- a/solution.py
+++ b/solution.py
@@ -206,17 +206,15 @@
     arrived(zz, ox, 1, c)
     forward(zz, ox, 1, 9)
     hash_rows(steps // 2, steps)
-    own[0] = sums(xc, 0, 0)
-    own[1] = sums(xc, 1, 0)
     arrived(oz, ox, 0, c)
     forward(oz, ox, 0, 12)
     give(2, ox, 0)
-    own[2] = sums(ox, 0, 0)
     arrived(oz, ox, 1, c)
     forward(oz, ox, 1, 13)
     give(3, ox, 1)
     chunks = ((xc, 0), (xc, 1), (ox, 0), (ox, 1))
-    own[3] = sums(ox, 1, 0)
+    for n, (b, k) in enumerate(chunks):
+        own[n] = sums(b, k, 0)
 
     for n, (b, k) in enumerate(chunks):
         exchange(n).wait_recv()

time: 47.9 us -> 45.5 us (0.950)
  Pallas kernels: 43.5 us -> 41 us
    pallas_call x1, Pallas kernels: 43.5 us -> 41 us  [fused(): pl.pallas_call(fused_kernel, out_shape=(jax.ShapeDtypeStruct((n_ex, FEATS...]
where the time goes in v6:
time: 45.5 us; the launch traced here: 45.3 us
  Pallas kernels  41 us (90%)
  local copies, waits for them, and re-layouts  2.36 us (5%)
  between operations  1.94 us (4%)
    pallas_call x1, Pallas kernels, fused(): pl.pallas_call(fused_kernel, out_shape=(jax.ShapeDtypeStruct((n_ex, FEATS...  41 us
    unnamed x4, local copies, waits for them, and re-layouts  2.36 us

profile of v6, /device:TPU:0, one launch (start us, length us, event | category | flops | bytes accessed | tf_op | source)
XLA Modules:
  0.0 45.3 jit_solution(9011557244652732774)
XLA Ops:
  1.9 0.0 copy-start
  1.9 1.0 %copy-done = bf16[96,2048]{1,0:T(8,128)(2,1)S(1)} copy-done((bf16[96,2048]{1,0:T(8,128)(2,1)S(1)}, bf16[96,2048]{1,0:T(8,128)(2,1)}, u32[]{:S(2)}) %copy-start) | copy-done | bytes 393240
  2.9 41.0 %shard_map.50 = (bf16[96,2048]{1,0:T(8,128)(2,1)S(1)}, f32[96,96]{1,0:T(8,128)S(1)}) custom-call(s32[1]{0:T(128)S(6)} %copy.7.salt_ref, s32[1]{0:T(128)S(6)} %copy.8.offset_ref, bf16[96,2048]{1,0:T(8,128)(2,1)S(1)} %copy-done), custom_call_target="tpu_custom_call" | custom-call | tf_op jit(solution)/shard_map/pallas_call | solution.py:279
  43.9 0.7 %copy.9 = bf16[2048,96]{0,1:T(8,128)(2,1)} copy(bf16[2048,96]{0,1:T(8,128)(2,1)S(1)} %bitcast.1) | data formatting | bytes 786432
  44.7 0.6 %copy.10 = f32[96,96]{1,0:T(8,128)} copy(f32[96,96]{1,0:T(8,128)S(1)} %get-tuple-element.9) | data formatting | bytes 73728
Async XLA Ops:
  1.9 1.0 %copy-start = (bf16[96,2048]{1,0:T(8,128)(2,1)S(1)}, bf16[96,2048]{1,0:T(8,128)(2,1)}, u32[]{:S(2)}) copy-start(bf16[96,2048]{1,0:T(8,128)(2,1)} %grads_ref.1) | copy-start | bytes 1179652
